TPU v7x, 128 devices: a whole 4x4x4 slice. The times are simulated.
128 devices in a mesh: group: 8 (over y, x_hi), blk: 16 (over x_lo, z, core).
Axes of the slice: x: 4 (x_hi: 2, x_lo: 2; x = x_hi * 2 + x_lo), y: 4, z: 4, core: 2. Of those that a mesh axis runs over, the one named last changes fastest.
Arguments:
- features: bfloat16 [131072, 512], P(('group', 'blk')), may hold values from -6 to 6
- tenant: int32 [131072, 1], P(('group', 'blk')), may hold values from 0 to 31; in each aligned block of 1024 rows (0 to 1023, 1024 to 2047, ...) at most 64 rows name the same one
- label: int32 [131072], P(('group', 'blk')), may hold values from 0 to 2047
- tenant_slot: int32 [32], replicated, may hold values from 0 to 31, each once
- sample: int32 [32, 16], P('group', 'blk'), may hold values from 0 to 7
- centres: bfloat16 [32, 16384, 512], P('group', 'blk'), may hold values from -6 to 6
Outputs:
- loss: float32 [131072], P(('group', 'blk'))
Inputs may be any that keep to these rules, and one draw needn't show every extreme that they name: The rows of one device name at most 64 rows of one tenant; some device's rows name some tenant exactly 64 times. `tenant_slot`: A permutation of the slots.
All inputs are finite; a program needn't handle non-finite values.
Results may differ from a plain program's by a relative error of at most 0.0003.
Values may be sent and summed in bfloat16 or wider, within the bound.
A program may use at most 128 MiB of HBM per device.

v0:
```python
import jax
import jax.numpy as jnp
from jax import lax
from jax.sharding import PartitionSpec as P

TILE = 128


logit_scale = 32.0
margin = 0.35
epsilon = 1e-06


def normalized(values):
    wide = values.astype(jnp.float32)
    return (wide * lax.rsqrt(jnp.sum(wide * wide, axis=-1, keepdims=True) + epsilon)).astype(
        jnp.bfloat16
    )


def targets_of(owners, columns, span):
    return (owners.astype(jnp.int32) - 1) * span + columns.astype(jnp.int32)


def partial_terms(rows_block, targets, kernel):
    cosine = jnp.einsum("trd,tcd->trc", rows_block, kernel, preferred_element_type=jnp.float32)
    columns = lax.broadcasted_iota(jnp.int32, (1, 1, kernel.shape[1]), 2)
    chosen = targets[:, :, None] == columns
    logits = logit_scale * (cosine - margin * chosen.astype(jnp.float32))
    totals = jnp.sum(jnp.exp(logits), axis=2)
    positive = jnp.sum(jnp.where(chosen, logits, 0.0), axis=2)
    return jnp.stack([totals, positive])


def body(features, tenant, label, tenant_slot, sample, centres):
    row_count = features.shape[0]
    width = features.shape[1]
    groups = lax.axis_size("group")
    ten_local = sample.shape[0]
    sample_tiles = sample.shape[1]
    stored_tiles = centres.shape[1] // TILE
    tenants = ten_local * groups
    capacity = max(2, 2 * row_count // tenants)
    span = sample_tiles * TILE
    slots_all = tenants * capacity
    unit = normalized(features)
    which = tenant[:, 0][:, None] == lax.broadcasted_iota(jnp.int32, (1, tenants), 1)
    slot = jnp.sum(jnp.where(which, tenant_slot[None, :], 0), axis=1)
    order = lax.broadcasted_iota(jnp.int32, (row_count,), 0)
    earlier = (slot[:, None] == slot[None, :]) & (order[:, None] > order[None, :])
    rank = jnp.sum(earlier.astype(jnp.int32), axis=1)
    position = slot * capacity + rank
    placing = (position[None, :] == lax.broadcasted_iota(jnp.int32, (slots_all, 1), 0)).astype(
        jnp.bfloat16
    )
    send_rows = jnp.dot(placing, unit, preferred_element_type=jnp.float32).astype(jnp.bfloat16)
    send_rows = send_rows.reshape(groups, ten_local, capacity, width)
    codes = jnp.stack([label // span + 1, label % span], axis=1).astype(jnp.bfloat16)
    send_codes = jnp.dot(placing, codes, preferred_element_type=jnp.float32).astype(jnp.bfloat16)
    owners_out = send_codes[:, 0].reshape(groups, ten_local, capacity)
    columns_out = send_codes[:, 1].reshape(groups, ten_local, capacity)
    arrived, owners, columns = (
        lax.all_to_all(send_rows, "group", split_axis=0, concat_axis=2, tiled=True),
        lax.all_to_all(owners_out, "group", split_axis=0, concat_axis=2, tiled=True),
        lax.all_to_all(columns_out, "group", split_axis=0, concat_axis=2, tiled=True),
    )
    arrived = arrived[0]
    owners = owners[0]
    columns = columns[0]
    targets = targets_of(owners, columns, span)
    stacked = centres.reshape(ten_local, stored_tiles, TILE, width)
    picked = jnp.take_along_axis(stacked, sample[:, :, None, None], axis=1)
    kernel = normalized(picked.reshape(ten_local, span, width))
    summed = partial_terms(arrived, targets, lax.all_gather(kernel, "blk", axis=1, tiled=True))
    valid = owners.astype(jnp.float32) > 0.5
    losses = jnp.where(valid, jnp.log(summed[0]) - summed[1], 0.0)
    returned = lax.all_to_all(losses[None], "group", split_axis=2, concat_axis=0, tiled=True)
    return returned.reshape(-1)[position]


def solution(mesh):
    return jax.shard_map(
        body,
        mesh=mesh,
        in_specs=(
            P(("group", "blk"), None),
            P(("group", "blk"), None),
            P(("group", "blk")),
            P(),
            P("group", "blk"),
            P("group", "blk", None),
        ),
        out_specs=P(("group", "blk")),
        check_vma=False,
    )
```

profile of v0, /device:TPU:1, one launch (start us, length us, event | category | flops | bytes accessed | tf_op | source)
XLA Modules:
  0.0 134.7 jit_solution(3805208119621128253)
XLA Ops:
  6.5 0.7 compare_select_fusion.1
  7.3 0.7 and_bitcast_fusion
  8.0 2.8 %gather_fusion.1 = bf16[4,128,512]{2,1,0:T(8,128)(2,1)S(1)} fusion(bf16[4,8,128,512]{3,2,1,0:T(8,128)(2,1)} %bitcast.45, s32[4]{0:T(128)S(1)} %or_bitcast_fusion), kind=kCustom, calls=%fused_computation.1 | custom fusion | bytes 1048608 | tf_op jit(solution)/shard_map/jit(take_along_axis)/gather | solution.py:72
  11.0 1.0 fusion.10
  12.1 0.7 fusion.15
  12.8 0.8 select_reduce_fusion.1
  14.2 1.5 %fusion.6 = bf16[2048,2]{0,1:T(2,128)(2,1)S(1)} fusion(s32[1024]{0:T(1024)S(1)} %multiply_add_fusion, bf16[1024,1]{0,1:T(2,128)(2,1)S(1)} %stack.13, bf16[1024,1]{0,1:T(2,128)(2,1)S(1)} %stack.12), kind=kOutput, calls=%fused_computation.17 | convolution fusion | flops 10498048 | bytes 16384 | tf_op jit(solution)/shard_map/dot_general | solution.py:59
  15.8 0.7 reshape.213
  16.5 7.5 %all-to-all-start = ((bf16[8,2,128]{2,1,0:T(2,128)(2,1)}), bf16[8,2,128]{2,1,0:T(2,128)(2,1)S(1)}, u32[]{:S(2)}, u32[]{:S(2)}) async-start(bf16[8,2,128]{2,1,0:T(2,128)(2,1)} %reshape.213), calls=%async_computation | async-start | bytes 8192 | tf_op jit(solution)/shard_map/all_to_all | solution.py:64
  24.3 0.7 reshape.215
  25.0 5.4 %all-to-all-done = bf16[8,2,128]{2,1,0:T(2,128)(2,1)S(1)} async-done(((bf16[8,2,128]{2,1,0:T(2,128)(2,1)}), bf16[8,2,128]{2,1,0:T(2,128)(2,1)S(1)}, u32[]{:S(2)}, u32[]{:S(2)}) %all-to-all-start) | async-done | bytes 4128 | tf_op jit(solution)/shard_map/all_to_all | solution.py:64
  30.4 3.2 %all-to-all-start.2 = ((bf16[8,2,128]{2,1,0:T(2,128)(2,1)}), bf16[8,2,128]{2,1,0:T(2,128)(2,1)S(1)}, u32[]{:S(2)}, u32[]{:S(2)}) async-start(bf16[8,2,128]{2,1,0:T(2,128)(2,1)} %reshape.215), calls=%async_computation.2 | async-start | bytes 8192 | tf_op jit(solution)/shard_map/all_to_all | solution.py:65
  33.6 3.8 %fusion.5 = bf16[2048,512]{1,0:T(8,128)(2,1)} fusion(s32[1024]{0:T(1024)S(1)} %multiply_add_fusion, bf16[1024,512]{1,0:T(8,128)(2,1)S(1)} %copy-done, f32[1024]{0:T(1024)S(1)} %add_rsqrt_fusion), kind=kOutput, calls=%fused_computation.14 | convolution fusion | flops 2152202240 | bytes 3153920 | tf_op jit(solution)/shard_map/dot_general | solution.py:56
  37.4 2.6 %all-to-all-done.2 = bf16[8,2,128]{2,1,0:T(2,128)(2,1)S(1)} async-done(((bf16[8,2,128]{2,1,0:T(2,128)(2,1)}), bf16[8,2,128]{2,1,0:T(2,128)(2,1)S(1)}, u32[]{:S(2)}, u32[]{:S(2)}) %all-to-all-start.2) | async-done | bytes 4128 | tf_op jit(solution)/shard_map/all_to_all | solution.py:65
  40.0 4.0 %all-to-all-start.1 = ((bf16[8,4,64,512]{3,2,1,0:T(8,128)(2,1)}), bf16[8,4,64,512]{3,2,1,0:T(8,128)(2,1)S(1)}, u32[]{:S(2)}, u32[]{:S(2)}) async-start(bf16[8,4,64,512]{3,2,1,0:T(8,128)(2,1)} %bitcast.40), calls=%async_computation.1 | async-start | bytes 4194304 | tf_op jit(solution)/shard_map/all_to_all | solution.py:63
  44.4 46.8 %all-to-all-done.1 = bf16[8,4,64,512]{3,2,1,0:T(8,128)(2,1)S(1)} async-done(((bf16[8,4,64,512]{3,2,1,0:T(8,128)(2,1)}), bf16[8,4,64,512]{3,2,1,0:T(8,128)(2,1)S(1)}, u32[]{:S(2)}, u32[]{:S(2)}) %all-to-all-start.1) | async-done | bytes 2097184 | tf_op jit(solution)/shard_map/all_to_all | solution.py:63
  91.2 1.6 %copy.18 = bf16[1,4,8,64,512]{4,3,2,1,0:T(8,128)(2,1)} copy(bf16[1,4,8,64,512]{4,3,1,2,0:T(8,128)(2,1)S(1)} %bitcast.39) | data formatting | bytes 4194304 | tf_op jit(solution)/shard_map/all_to_all | solution.py:63
  92.8 10.5 %exponential_reduce_fusion = (f32[4,512]{1,0:T(4,128)S(1)}, f32[4,512]{1,0:T(4,128)S(1)}) fusion(s32[4,512]{1,0:T(4,128)S(1)} %add.112, bf16[4,512,512]{2,1,0:T(8,128)(2,1)} %bitcast.41, bf16[4,2048,512]{2,1,0:T(8,128)(2,1)} %all-gather.2.cloned.1.call-done), kind=kOutput, calls=%fused_computation.3 | convolution fusion | flops 4324323328 | bytes 10510336 | tf_op jit(solution)/shard_map/trd,tcd->trc/dot_general | solution.py:26
  104.1 1.3 reduce.4
  105.4 0.8 reshape.217
  106.1 3.3 %all-to-all-start.3 = ((f32[8,1,256]{2,1,0:T(1,128)}), f32[8,1,256]{2,1,0:T(1,128)S(1)}, u32[]{:S(2)}, u32[]{:S(2)}) async-start(f32[8,1,256]{2,1,0:T(1,128)} %reshape.217), calls=%async_computation.3 | async-start | bytes 16384 | tf_op jit(solution)/shard_map/all_to_all | solution.py:77
  109.5 6.5 %all-to-all-done.3 = f32[8,1,256]{2,1,0:T(1,128)S(1)} async-done(((f32[8,1,256]{2,1,0:T(1,128)}), f32[8,1,256]{2,1,0:T(1,128)S(1)}, u32[]{:S(2)}, u32[]{:S(2)}) %all-to-all-start.3) | async-done | bytes 8224 | tf_op jit(solution)/shard_map/all_to_all | solution.py:77
  115.9 0.7 reduce.5
  117.3 10.5 %gather_fusion = f32[1024]{0:T(1024)} fusion(f32[2048]{0:T(1024)S(1)} %reshape.189, s32[1024]{0:T(1024)S(1)} %broadcast_clamp_fusion), kind=kCustom, calls=%fused_computation | custom fusion | bytes 12288 | tf_op jit(solution)/shard_map/gather | solution.py:78
  (35 shorter events, 3.1 us)
Async XLA Ops:
  6.5 17.4 %copy-start = (bf16[1024,512]{1,0:T(8,128)(2,1)S(1)}, bf16[1024,512]{1,0:T(8,128)(2,1)}, u32[]{:S(2)}) copy-start(bf16[1024,512]{1,0:T(8,128)(2,1)} %param.6) | copy-start | bytes 3145732
  6.5 86.3 %all-gather.2.cloned.1.call-start = ((), (), s32[]{:S(2)}) async-start(), calls=%async_computation.4 | async-start | bytes 8912896 | tf_op jit(solution)/shard_map/all_gather | solution.py:74
  16.5 13.9 %all-to-all-start = ((bf16[8,2,128]{2,1,0:T(2,128)(2,1)}), bf16[8,2,128]{2,1,0:T(2,128)(2,1)S(1)}, u32[]{:S(2)}, u32[]{:S(2)}) async-start(bf16[8,2,128]{2,1,0:T(2,128)(2,1)} %reshape.213), calls=%async_computation | async-start | bytes 8192 | tf_op jit(solution)/shard_map/all_to_all | solution.py:64
  30.4 9.7 %all-to-all-start.2 = ((bf16[8,2,128]{2,1,0:T(2,128)(2,1)}), bf16[8,2,128]{2,1,0:T(2,128)(2,1)S(1)}, u32[]{:S(2)}, u32[]{:S(2)}) async-start(bf16[8,2,128]{2,1,0:T(2,128)(2,1)} %reshape.215), calls=%async_computation.2 | async-start | bytes 8192 | tf_op jit(solution)/shard_map/all_to_all | solution.py:65
  40.0 51.2 %all-to-all-start.1 = ((bf16[8,4,64,512]{3,2,1,0:T(8,128)(2,1)}), bf16[8,4,64,512]{3,2,1,0:T(8,128)(2,1)S(1)}, u32[]{:S(2)}, u32[]{:S(2)}) async-start(bf16[8,4,64,512]{3,2,1,0:T(8,128)(2,1)} %bitcast.40), calls=%async_computation.1 | async-start | bytes 4194304 | tf_op jit(solution)/shard_map/all_to_all | solution.py:63
  106.1 9.8 %all-to-all-start.3 = ((f32[8,1,256]{2,1,0:T(1,128)}), f32[8,1,256]{2,1,0:T(1,128)S(1)}, u32[]{:S(2)}, u32[]{:S(2)}) async-start(f32[8,1,256]{2,1,0:T(1,128)} %reshape.217), calls=%async_computation.3 | async-start | bytes 16384 | tf_op jit(solution)/shard_map/all_to_all | solution.py:77
Sparse Core Ops, SparseCore 0:
  12.2 75.3 all-gather.1
where the time goes:
time: 136 us; the launch traced here: 135 us
  waiting for transfers between devices  61.3 us (45%)
  local copies, waits for them, and re-layouts  19 us (14%)
  starting transfers between devices  18 us (13%)
  matrix products  15.8 us (12%)
  between operations  13.5 us (10%)
  other arithmetic  7.06 us (5%)
    all_to_all x1, waiting for transfers between devices, body(): lax.all_to_all(send_rows, 'group', split_axis=0, concat_axis=2, tiled=True)  46.8 us
    gather x1, local copies, waits for them, and re-layouts, body(): return returned.reshape(-1)[position]  10.5 us
    dot_general x1, matrix products, partial_terms(): jnp.einsum('trd,tcd->trc', rows_block, kernel, preferred_element_type=jnp...  10.5 us
    all_to_all x1, starting transfers between devices, body(): lax.all_to_all(owners_out, 'group', split_axis=0, concat_axis=2, tiled=True)  7.48 us
    all_to_all x1, waiting for transfers between devices, body(): lax.all_to_all(losses[None], 'group', split_axis=2, concat_axis=0, tiled=...  6.45 us
    all_to_all x1, waiting for transfers between devices, body(): lax.all_to_all(owners_out, 'group', split_axis=0, concat_axis=2, tiled=True)  5.38 us
    all_to_all x1, starting transfers between devices, body(): lax.all_to_all(send_rows, 'group', split_axis=0, concat_axis=2, tiled=True)  3.96 us
    dot_general x1, matrix products, body(): jnp.dot(placing, unit, preferred_element_type=jnp.float32)  3.82 us
  transfers between devices with their start and end apart: 5, of which 4 were waited for; matrix products, arithmetic and copies ran while one was open for 8% of the time, Pallas kernels for 0%

commit v1 on v0

v1 whole, which is shorter than its diff:
```python
import functools
import jax
import jax.numpy as jnp
from jax import lax
from jax.experimental import pallas as pl
from jax.experimental.pallas import tpu as pltpu
from jax.sharding import PartitionSpec as P

MESH = pl.DeviceIdType.MESH
TILE = 128
WIDTH = 512
ROWS = 1024
CAP = 64
SLOTS = 32
LANES = 128
CODE = 4 * CAP
BLOCK = CODE + 16
logit_scale = 32.0
margin = 0.35
epsilon = 1e-06
LOG2E = 1.4426950408889634


def hops(d):
    return min(d, 4 - d)


CHIPS = sorted(
    [(dx, dy) for dx in range(4) for dy in range(4)],
    key=lambda d: (-hops(d[0]) - hops(d[1]), (d[0] + d[1]) % 4),
)
SELF_CHIP = CHIPS.index((0, 0))
SELF = 2 * SELF_CHIP


def normalized(values, scale):
    wide = values.astype(jnp.float32)
    inverse = lax.rsqrt(jnp.sum(wide * wide, axis=-1, keepdims=True) + epsilon)
    return (wide * inverse * scale).astype(jnp.bfloat16)


def kernel(
    slot_ref, sample_ref, tenant_ref, label_ref, feat_hbm, cent_hbm, out_ref,
    cent0, cent1, cent2, cent3, unit, snd, rcv, tiles, kern, acc_e, acc_p, lsnd, ret,
    in_sem, row_ss, row_rs, quad_ss, quad_rs, z_ss, z_rs, loss_ss, loss_rs,
):
    group, blk = lax.axis_index("group"), lax.axis_index("blk")
    y, xh = lax.div(group, 2), lax.rem(group, 2)
    xl, z, c = lax.div(blk, 8), lax.rem(lax.div(blk, 2), 4), lax.rem(blk, 2)
    x = xh * 2 + xl

    def device(x_, y_, z_, c_):
        return (y_ * 2 + lax.div(x_, 2), lax.rem(x_, 2) * 8 + z_ * 2 + c_)

    def row_peer(o):
        dx, dy = CHIPS[o // 2]
        return device(lax.rem(x + dx, 4), lax.rem(y + dy, 4), z, lax.rem(c + o % 2, 2))

    def row_source(o):
        dx, dy = CHIPS[o // 2]
        return device(lax.rem(x + 4 - dx, 4), lax.rem(y + 4 - dy, 4), z, lax.rem(c + o % 2, 2))

    def quad_peer(q):
        return device(xh * 2 + lax.rem(xl + q // 2, 2), y, z, lax.rem(c + q % 2, 2))

    def z_peer(d):
        return device(x, y, lax.rem(z + d, 4), c)

    cents = (cent0, cent1, cent2, cent3)
    loads = []
    for q in range(4):
        t = lax.rem(xl + q // 2, 2) * 2 + lax.rem(c + q % 2, 2)
        loads.append(pltpu.make_async_copy(cent_hbm.at[t], cents[q], in_sem.at[q]))
        loads[q].start()
    feat_load = pltpu.make_async_copy(feat_hbm, unit, in_sem.at[4])
    feat_load.start()

    barrier = pltpu.get_barrier_semaphore()
    others = [o for o in range(SLOTS) if o != SELF]
    for o in others:
        pl.semaphore_signal(barrier, inc=1, device_id=row_peer(o), device_id_type=MESH)
    for d in (1, 2, 3):
        pl.semaphore_signal(barrier, inc=1, device_id=z_peer(d), device_id_type=MESH)

    for q in range(4):
        t = lax.rem(xl + q // 2, 2) * 2 + lax.rem(c + q % 2, 2)
        loads[q].wait()
        block = normalized(cents[q][sample_ref[t]], logit_scale)
        if q == 0:
            kern[0, 0] = block
        else:
            tiles[q - 1] = block

    pl.semaphore_wait(barrier, len(others) + 3)

    quad = []
    for q in (2, 3, 1):
        quad.append(
            pltpu.make_async_remote_copy(
                src_ref=tiles.at[q - 1], dst_ref=kern.at[0, q], send_sem=quad_ss.at[q - 1],
                recv_sem=quad_rs.at[q - 1], device_id=quad_peer(q), device_id_type=MESH,
            )
        )
        quad[-1].start()

    z_copies = {}

    def along_z(q):
        for d in (1, 3, 2):
            z_copies[d, q] = pltpu.make_async_remote_copy(
                src_ref=kern.at[0, q], dst_ref=kern.at[d, q], send_sem=z_ss.at[d - 1, q],
                recv_sem=z_rs.at[d - 1, q], device_id=z_peer(d), device_id_type=MESH,
            )
            z_copies[d, q].start()

    along_z(0)

    tenant = tenant_ref[...]
    slot = jnp.zeros_like(tenant)
    for n in range(SLOTS):
        slot = jnp.where(tenant == n, slot_ref[n], slot)
    y_to, xh_to = lax.shift_right_logical(slot, 3), lax.shift_right_logical(slot, 2) & 1
    x_to, c_to = xh_to * 2 + (lax.shift_right_logical(slot, 1) & 1), slot & 1
    dx, dy, dc = (x_to - x + 4) & 3, (y_to - y + 4) & 3, (c_to + c) & 1
    chip = jnp.zeros_like(slot)
    for n, (a, b) in enumerate(CHIPS):
        chip = jnp.where((dx == a) & (dy == b), n, chip)
    order = chip * 2 + dc
    member = jnp.concatenate(
        [(order == n).astype(jnp.float32) for n in range(SLOTS)], axis=0
    )
    member16 = member.astype(jnp.bfloat16)
    i0 = lax.broadcasted_iota(jnp.int32, (LANES, LANES), 0)
    i1 = lax.broadcasted_iota(jnp.int32, (LANES, LANES), 1)
    before = (i0 < i1).astype(jnp.float32).astype(jnp.bfloat16)
    within = jnp.dot(member16, before, preferred_element_type=jnp.float32)
    ones = jnp.ones((LANES, LANES), jnp.bfloat16)
    totals = jnp.dot(member16, ones, preferred_element_type=jnp.float32).astype(jnp.bfloat16)
    j0 = lax.broadcasted_iota(jnp.int32, (8 * SLOTS, 8 * SLOTS), 0)
    j1 = lax.broadcasted_iota(jnp.int32, (8 * SLOTS, 8 * SLOTS), 1)
    above = ((j1 < j0) & (lax.shift_right_logical(j0, 3) == lax.shift_right_logical(j1, 3)))
    above = above.astype(jnp.float32).astype(jnp.bfloat16)
    earlier = jnp.dot(above, totals, preferred_element_type=jnp.float32)
    ranks = (member * (within + earlier)).reshape(SLOTS, 8, LANES)
    rank = jnp.sum(ranks, axis=0).astype(jnp.int32)
    position = order * CAP + rank

    def as_row(v):
        return jnp.concatenate([v[r : r + 1, :] for r in range(8)], axis=1)

    position_row = as_row(position)
    label = as_row(label_ref[...])
    code_at = lax.broadcasted_iota(jnp.int32, (16, ROWS), 0)
    codes = jnp.where(
        code_at == 0, lax.shift_right_logical(label, 7), jnp.where(code_at == 1, label & 127, 0)
    ).astype(jnp.float32).astype(jnp.bfloat16)

    feat_load.wait()
    unit[...] = normalized(unit[...], 1.0)

    rows = {}
    iota_slot = lax.broadcasted_iota(jnp.int32, (4 * CAP, 1), 0)
    for k in range(8):
        placing = (position_row == iota_slot + k * 4 * CAP).astype(jnp.float32).astype(jnp.bfloat16)
        placed = jnp.dot(placing, unit[...], preferred_element_type=jnp.float32).astype(jnp.bfloat16)
        coded = lax.dot_general(
            codes, placing, (((1,), (1,)), ((), ())), preferred_element_type=jnp.float32
        ).astype(jnp.bfloat16)
        for a in range(4):
            o = 4 * k + a
            to = rcv if o == SELF else snd
            for f in range(4):
                to[o, f * CAP : (f + 1) * CAP, :] = placed[
                    a * CAP : (a + 1) * CAP, f * LANES : (f + 1) * LANES
                ]
            to[o, CODE:BLOCK, :] = coded[:, (a // 2) * LANES : (a // 2 + 1) * LANES]
        for a in (0, 2, 1, 3):
            o = 4 * k + a
            if o != SELF:
                rows[o] = pltpu.make_async_remote_copy(
                    src_ref=snd.at[o], dst_ref=rcv.at[o], send_sem=row_ss.at[o],
                    recv_sem=row_rs.at[o], device_id=row_peer(o), device_id_type=MESH,
                )
                rows[o].start()
        if k == 0:
            quad[2].wait()
            along_z(1)
        if k == 4:
            quad[0].wait()
            along_z(2)
        if k == 5:
            quad[1].wait()
            along_z(3)

    acc_e[...] = jnp.zeros_like(acc_e)
    acc_p[...] = jnp.zeros_like(acc_p)
    lane = lax.broadcasted_iota(jnp.int32, (1, LANES), 1)
    in_tile = lax.broadcasted_iota(jnp.int32, (TILE, 4 * CAP), 0).astype(jnp.float32)

    def targets(k):
        halves = []
        for h in range(2):
            first = rcv[4 * k + 2 * h, CODE:BLOCK, :].astype(jnp.float32)
            second = rcv[4 * k + 2 * h + 1, CODE:BLOCK, :].astype(jnp.float32)
            both = jnp.where(lane < CAP, first, second)
            halves.append(both[0:1, :] * float(TILE) + both[1:2, :])
        return jnp.concatenate(halves, axis=1)

    def group_rows(k):
        return jnp.concatenate(
            [
                jnp.concatenate(
                    [rcv[4 * k + a, f * CAP : (f + 1) * CAP, :] for f in range(4)], axis=1
                )
                for a in range(4)
            ],
            axis=0,
        )

    def step(k, j):
        target = targets(k)
        block = group_rows(k)

        def half(h, carry):
            for q in range(2):
                cosine = lax.dot_general(
                    kern[j, 2 * h + q], block, (((1,), (1,)), ((), ())),
                    preferred_element_type=jnp.float32,
                )
                owner = (lax.rem(xl + h, 2) * 4 + lax.rem(z - j + 4, 4)) * 2 + lax.rem(c + q, 2)
                hit = in_tile == target - (owner * TILE).astype(jnp.float32)
                e = jnp.where(hit, 0.0, jnp.exp2(cosine * LOG2E))
                p = jnp.where(hit, cosine, 0.0)
                acc_e[k] += jnp.sum(e.reshape(TILE // 8, 8, 4 * CAP), axis=0)
                acc_p[k] += jnp.sum(p.reshape(TILE // 8, 8, 4 * CAP), axis=0)
            return carry

        lax.fori_loop(0, 2, half, 0)

    def steps(ks, js):
        for j in js:
            lax.fori_loop(ks[0], ks[1], lambda k, carry: (step(k, j), carry)[1], 0)

    def arrived(k):
        for a in range(4):
            if 4 * k + a != SELF:
                rows[4 * k + a].wait_recv()

    def z_arrived(d):
        for q in range(4):
            z_copies[d, q].wait_recv()

    losses = {}

    def finish(k):
        positive = jnp.sum(acc_p[k], axis=0, keepdims=True) - logit_scale * margin
        total = jnp.sum(acc_e[k], axis=0, keepdims=True) + jnp.exp(positive)
        loss = jnp.log(total) - positive
        for h in range(2):
            lsnd[2 * k + h] = jnp.broadcast_to(loss[:, h * LANES : (h + 1) * LANES], (8, LANES))
        for a in range(4):
            o = 4 * k + a
            if o == SELF:
                ret[o] = jnp.broadcast_to(loss[:, (a // 2) * LANES : (a // 2 + 1) * LANES], (8, LANES))
            else:
                losses[o] = pltpu.make_async_remote_copy(
                    src_ref=lsnd.at[o // 2], dst_ref=ret.at[o], send_sem=loss_ss.at[o],
                    recv_sem=loss_rs.at[o], device_id=row_source(o), device_id_type=MESH,
                )
                losses[o].start()

    for k in range(4):
        arrived(k)
        steps((k, k + 1), (0,))
    z_arrived(1)
    z_arrived(3)
    steps((0, 4), (1, 3))
    for k in range(4, 6):
        arrived(k)
        steps((k, k + 1), (0, 1, 3))
    z_arrived(2)
    steps((0, 6), (2,))
    for k in range(6):
        finish(k)
    for k in range(6, 8):
        arrived(k)
        steps((k, k + 1), (0, 1, 3, 2))
        finish(k)

    at = (order & 1) * CAP + rank
    loss_out = jnp.zeros((8, LANES), jnp.float32)
    for o in range(SLOTS):
        if o != SELF:
            losses[o].wait_recv()
        mine = jnp.take_along_axis(ret[o], at, axis=1)
        loss_out = jnp.where(order == o, mine, loss_out)
    out_ref[...] = loss_out

    for copy in [*rows.values(), *z_copies.values(), *losses.values()]:
        copy.wait_send()


def body(features, tenant, label, tenant_slot, sample, centres):
    vmem = pl.BlockSpec(memory_space=pltpu.VMEM)
    smem = pl.BlockSpec(memory_space=pltpu.SMEM)
    hbm = pl.BlockSpec(memory_space=pl.ANY)
    bf16, f32 = jnp.bfloat16, jnp.float32
    dma = pltpu.SemaphoreType.DMA
    out = pl.pallas_call(
        kernel,
        out_shape=jax.ShapeDtypeStruct((8, LANES), f32),
        in_specs=[smem, smem, vmem, vmem, hbm, hbm],
        out_specs=vmem,
        scratch_shapes=[
            *[pltpu.VMEM((8, TILE, WIDTH), bf16) for _ in range(4)],
            pltpu.VMEM((ROWS, WIDTH), bf16),
            pltpu.VMEM((SLOTS, BLOCK, LANES), bf16),
            pltpu.VMEM((SLOTS, BLOCK, LANES), bf16),
            pltpu.VMEM((3, TILE, WIDTH), bf16),
            pltpu.VMEM((4, 4, TILE, WIDTH), bf16),
            pltpu.VMEM((8, 8, 4 * CAP), f32),
            pltpu.VMEM((8, 8, 4 * CAP), f32),
            pltpu.VMEM((16, 8, LANES), f32),
            pltpu.VMEM((SLOTS, 8, LANES), f32),
            dma((5,)), dma((SLOTS,)), dma((SLOTS,)), dma((3,)), dma((3,)),
            dma((3, 4)), dma((3, 4)), dma((SLOTS,)), dma((SLOTS,)),
        ],
        compiler_params=pltpu.CompilerParams(
            collective_id=0, has_side_effects=True, vmem_limit_bytes=48 << 20
        ),
    )(
        tenant_slot, sample.reshape(4), tenant.reshape(8, LANES), label.reshape(8, LANES),
        features, centres.reshape(4, 8, TILE, WIDTH),
    )
    return out.reshape(ROWS)


def solution(mesh):
    return jax.shard_map(
        body,
        mesh=mesh,
        in_specs=(
            P(("group", "blk"), None),
            P(("group", "blk"), None),
            P(("group", "blk")),
            P(),
            P("group", "blk"),
            P("group", "blk", None),
        ),
        out_specs=P(("group", "blk")),
        check_vma=False,
    )
```

time: 136 us -> 66.8 us (0.49)
  waiting for transfers between devices: 61.3 us -> 0 us
  Pallas kernels: 0 us -> 59.8 us
  starting transfers between devices: 18 us -> 0 us
  matrix products: 15.8 us -> 0 us
  between operations: 13.5 us -> 0.02 us
  local copies, waits for them, and re-layouts: 19 us -> 6.69 us
  other arithmetic: 7.06 us -> 0 us
    all_to_all x4 -> x0, waiting for transfers between devices: 61.3 us -> none  [the longest x1 46.8 us: body(): lax.all_to_all(send_rows, 'group', split_axis=0, concat_axis=2, tiled=True)]
    pallas_call x0 -> x1, Pallas kernels: none -> 59.8 us  [body(): pl.pallas_call(kernel, out_shape=jax.ShapeDtypeStruct((8, LANES), f32), i...]
    all_to_all x4 -> x0, starting transfers between devices: 18 us -> none  [the longest x1 7.48 us: body(): lax.all_to_all(owners_out, 'group', split_axis=0, concat_axis=2, tiled=True)]
    dot_general x3 -> x0, matrix products: 15.8 us -> none  [the longest x1 10.5 us: partial_terms(): jnp.einsum('trd,tcd->trc', rows_block, kernel, preferred_element_type=jnp...]
    gather x2 -> x0, local copies, waits for them, and re-layouts: 13.3 us -> none  [the longest x1 10.5 us: body(): return returned.reshape(-1)[position]]
    unnamed x10 -> x13, local copies, waits for them, and re-layouts: 3.28 us -> 6.69 us
    reduce_sum x4 -> x0, other arithmetic: 1.87 us -> none  [the longest x1 0.79 us: body(): slot = jnp.sum(jnp.where(which, tenant_slot[None, :], 0), axis=1)]
    all_to_all x2 -> x0, local copies, waits for them, and re-layouts: 1.76 us -> none  [the longest x1 1.62 us: body(): lax.all_to_all(send_rows, 'group', split_axis=0, concat_axis=2, tiled=True)]
  transfers between devices with their start and end apart: 5 -> 0, of which waited for: 4 -> 0; matrix products, arithmetic and copies ran while one was open for 8% -> 0% of each run, Pallas kernels for 0% -> 0%
where the time goes in v1:
time: 66.8 us; the launch traced here: 66.5 us
  Pallas kernels  59.8 us (90%)
  local copies, waits for them, and re-layouts  6.69 us (10%)
    pallas_call x1, Pallas kernels, body(): pl.pallas_call(kernel, out_shape=jax.ShapeDtypeStruct((8, LANES), f32), i...  59.8 us
    unnamed x13, local copies, waits for them, and re-layouts  6.69 us

profile of v1, /device:TPU:1, one launch (start us, length us, event | category | flops | bytes accessed | tf_op | source)
XLA Modules:
  0.0 66.5 jit_solution(7611388042575336473)
XLA Ops:
  0.0 0.0 copy-start
  0.0 2.2 %copy-done = bf16[4,1024,512]{2,1,0:T(8,128)(2,1)S(1)} copy-done((bf16[4,1024,512]{2,1,0:T(8,128)(2,1)S(1)}, bf16[4,1024,512]{2,1,0:T(8,128)(2,1)}, u32[]{:S(2)}) %copy-start) | copy-done | bytes 4194328
  2.2 0.0 copy-start.1
  2.2 1.2 %copy-done.1 = bf16[1024,512]{1,0:T(8,128)(2,1)S(1)} copy-done((bf16[1024,512]{1,0:T(8,128)(2,1)S(1)}, bf16[1024,512]{1,0:T(8,128)(2,1)}, u32[]{:S(2)}) %copy-start.1) | copy-done | bytes 1048600
  3.4 0.0 copy-start.2
  3.4 0.7 %copy-done.2 = s32[1024,1]{0,1:T(1,128)S(1)} copy-done((s32[1024,1]{0,1:T(1,128)S(1)}, s32[1024,1]{0,1:T(1,128)}, u32[]{:S(2)}) %copy-start.2) | copy-done | bytes 4120
  4.1 0.0 copy-start.3
  4.1 0.7 %copy-done.3 = s32[1024]{0:T(1024)S(1)} copy-done((s32[1024]{0:T(1024)S(1)}, s32[1024]{0:T(1024)}, u32[]{:S(2)}) %copy-start.3) | copy-done | bytes 4120
  4.8 0.0 copy-start.4
  4.8 0.7 copy-done.4
  5.4 0.0 copy-start.5
  5.4 0.7 copy-done.5
  6.1 59.8 %shard_map.64 = f32[8,128]{1,0:T(8,128)S(1)} custom-call(s32[32]{0:T(128)S(1)} %copy-done.4, s32[4]{0:T(128)S(1)} %bitcast.9, s32[8,128]{1,0:T(8,128)S(1)} %bitcast.7, s32[8,128]{1,0:T(8,128)S(1)} %bitcast.8, bf16[1024,512]{1,0:T(8,128)(2,1)S(1)} %copy-done.1, bf16[4,8,128,512]{3,2,1,0:T(8,128)(2,1)S(1)} %bitcast.5), custom_call_target="tpu_custom_call" | custom-call | tf_op jit(solution)/shard_map/pallas_call | solution.py:309
  65.9 0.6 copy.8
Async XLA Ops:
  0.0 2.2 %copy-start = (bf16[4,1024,512]{2,1,0:T(8,128)(2,1)S(1)}, bf16[4,1024,512]{2,1,0:T(8,128)(2,1)}, u32[]{:S(2)}) copy-start(bf16[4,1024,512]{2,1,0:T(8,128)(2,1)} %param.11) | copy-start | bytes 12582916
  2.2 1.2 %copy-start.1 = (bf16[1024,512]{1,0:T(8,128)(2,1)S(1)}, bf16[1024,512]{1,0:T(8,128)(2,1)}, u32[]{:S(2)}) copy-start(bf16[1024,512]{1,0:T(8,128)(2,1)} %feat_hbm.1) | copy-start | bytes 3145732
  3.4 0.7 %copy-start.2 = (s32[1024,1]{0,1:T(1,128)S(1)}, s32[1024,1]{0,1:T(1,128)}, u32[]{:S(2)}) copy-start(s32[1024,1]{0,1:T(1,128)} %param.7) | copy-start | bytes 12292
  4.1 0.7 %copy-start.3 = (s32[1024]{0:T(1024)S(1)}, s32[1024]{0:T(1024)}, u32[]{:S(2)}) copy-start(s32[1024]{0:T(1024)} %param.8) | copy-start | bytes 12292
  4.8 0.7 copy-start.4
  5.4 0.7 copy-start.5

commit v2 on v1

--- a/solution.py
+++ b/solution.py
@@ -40,8 +40,8 @@
 
 
 def kernel(
-    slot_ref, sample_ref, tenant_ref, label_ref, feat_hbm, cent_hbm, out_ref,
-    cent0, cent1, cent2, cent3, unit, snd, rcv, tiles, kern, acc_e, acc_p, lsnd, ret,
+    slot_hbm, sample_hbm, tenant_hbm, label_hbm, feat_hbm, cent_hbm, out_ref,
+    slot_ref, sample_ref, tenant_ref, label_ref, cent0, cent1, cent2, cent3, unit, snd, rcv, tiles, kern, acc_e, acc_p, lsnd, ret,
     in_sem, row_ss, row_rs, quad_ss, quad_rs, z_ss, z_rs, loss_ss, loss_rs,
 ):
     group, blk = lax.axis_index("group"), lax.axis_index("blk")
@@ -68,6 +68,14 @@
 
     cents = (cent0, cent1, cent2, cent3)
     loads = []
+    small = [
+        pltpu.make_async_copy(sample_hbm, sample_ref, in_sem.at[5]),
+        pltpu.make_async_copy(slot_hbm, slot_ref, in_sem.at[6]),
+        pltpu.make_async_copy(tenant_hbm, tenant_ref, in_sem.at[7]),
+        pltpu.make_async_copy(label_hbm, label_ref, in_sem.at[8]),
+    ]
+    for load in small:
+        load.start()
     for q in range(4):
         t = lax.rem(xl + q // 2, 2) * 2 + lax.rem(c + q % 2, 2)
         loads.append(pltpu.make_async_copy(cent_hbm.at[t], cents[q], in_sem.at[q]))
@@ -82,39 +90,8 @@
     for d in (1, 2, 3):
         pl.semaphore_signal(barrier, inc=1, device_id=z_peer(d), device_id_type=MESH)
 
-    for q in range(4):
-        t = lax.rem(xl + q // 2, 2) * 2 + lax.rem(c + q % 2, 2)
-        loads[q].wait()
-        block = normalized(cents[q][sample_ref[t]], logit_scale)
-        if q == 0:
-            kern[0, 0] = block
-        else:
-            tiles[q - 1] = block
-
-    pl.semaphore_wait(barrier, len(others) + 3)
-
-    quad = []
-    for q in (2, 3, 1):
-        quad.append(
-            pltpu.make_async_remote_copy(
-                src_ref=tiles.at[q - 1], dst_ref=kern.at[0, q], send_sem=quad_ss.at[q - 1],
-                recv_sem=quad_rs.at[q - 1], device_id=quad_peer(q), device_id_type=MESH,
-            )
-        )
-        quad[-1].start()
-
-    z_copies = {}
-
-    def along_z(q):
-        for d in (1, 3, 2):
-            z_copies[d, q] = pltpu.make_async_remote_copy(
-                src_ref=kern.at[0, q], dst_ref=kern.at[d, q], send_sem=z_ss.at[d - 1, q],
-                recv_sem=z_rs.at[d - 1, q], device_id=z_peer(d), device_id_type=MESH,
-            )
-            z_copies[d, q].start()
-
-    along_z(0)
-
+    for load in small[1:]:
+        load.wait()
     tenant = tenant_ref[...]
     slot = jnp.zeros_like(tenant)
     for n in range(SLOTS):
@@ -158,6 +135,35 @@
     feat_load.wait()
     unit[...] = normalized(unit[...], 1.0)
 
+
+    quad = {}
+    z_copies = {}
+
+    def along_z(q):
+        for d in (1, 3, 2):
+            z_copies[d, q] = pltpu.make_async_remote_copy(
+                src_ref=kern.at[0, q], dst_ref=kern.at[d, q], send_sem=z_ss,
+                recv_sem=z_rs.at[d - 1], device_id=z_peer(d), device_id_type=MESH,
+            )
+            z_copies[d, q].start()
+
+    def own_tiles():
+        small[0].wait()
+        for q in (2, 3, 0, 1):
+            t = lax.rem(xl + q // 2, 2) * 2 + lax.rem(c + q % 2, 2)
+            loads[q].wait()
+            block = normalized(cents[q][sample_ref[t]], logit_scale)
+            if q == 0:
+                kern[0, 0] = block
+                along_z(0)
+                continue
+            tiles[q - 1] = block
+            quad[q] = pltpu.make_async_remote_copy(
+                src_ref=tiles.at[q - 1], dst_ref=kern.at[0, q], send_sem=quad_ss.at[q - 1],
+                recv_sem=quad_rs.at[q - 1], device_id=quad_peer(q), device_id_type=MESH,
+            )
+            quad[q].start()
+
     rows = {}
     iota_slot = lax.broadcasted_iota(jnp.int32, (4 * CAP, 1), 0)
     for k in range(8):
@@ -174,22 +180,26 @@
                     a * CAP : (a + 1) * CAP, f * LANES : (f + 1) * LANES
                 ]
             to[o, CODE:BLOCK, :] = coded[:, (a // 2) * LANES : (a // 2 + 1) * LANES]
+        if k == 0:
+            pl.semaphore_wait(barrier, len(others) + 3)
         for a in (0, 2, 1, 3):
             o = 4 * k + a
             if o != SELF:
                 rows[o] = pltpu.make_async_remote_copy(
-                    src_ref=snd.at[o], dst_ref=rcv.at[o], send_sem=row_ss.at[o],
-                    recv_sem=row_rs.at[o], device_id=row_peer(o), device_id_type=MESH,
+                    src_ref=snd.at[o], dst_ref=rcv.at[o], send_sem=row_ss,
+                    recv_sem=row_rs.at[k], device_id=row_peer(o), device_id_type=MESH,
                 )
                 rows[o].start()
         if k == 0:
+            own_tiles()
+        if k == 1:
+            quad[1].wait()
+            along_z(1)
+        if k == 5:
             quad[2].wait()
-            along_z(1)
-        if k == 4:
-            quad[0].wait()
             along_z(2)
-        if k == 5:
-            quad[1].wait()
+        if k == 6:
+            quad[3].wait()
             along_z(3)
 
     acc_e[...] = jnp.zeros_like(acc_e)
@@ -221,34 +231,34 @@
         target = targets(k)
         block = group_rows(k)
 
-        def half(h, carry):
-            for q in range(2):
-                cosine = lax.dot_general(
-                    kern[j, 2 * h + q], block, (((1,), (1,)), ((), ())),
-                    preferred_element_type=jnp.float32,
-                )
-                owner = (lax.rem(xl + h, 2) * 4 + lax.rem(z - j + 4, 4)) * 2 + lax.rem(c + q, 2)
-                hit = in_tile == target - (owner * TILE).astype(jnp.float32)
-                e = jnp.where(hit, 0.0, jnp.exp2(cosine * LOG2E))
-                p = jnp.where(hit, cosine, 0.0)
-                acc_e[k] += jnp.sum(e.reshape(TILE // 8, 8, 4 * CAP), axis=0)
-                acc_p[k] += jnp.sum(p.reshape(TILE // 8, 8, 4 * CAP), axis=0)
-            return carry
-
-        lax.fori_loop(0, 2, half, 0)
+        logits = lax.dot_general(
+            kern[j].reshape(4 * TILE, WIDTH), block, (((1,), (1,)), ((), ())),
+            preferred_element_type=jnp.float32,
+        )
+        sum_e, sum_p = acc_e[k], acc_p[k]
+        for q in range(4):
+            logit = logits[q * TILE : (q + 1) * TILE]
+            owner = (lax.rem(xl + q // 2, 2) * 4 + lax.rem(z - j + 4, 4)) * 2 + lax.rem(c + q % 2, 2)
+            hit = in_tile == target - (owner * TILE).astype(jnp.float32)
+            e = jnp.where(hit, 0.0, jnp.exp2(logit * LOG2E))
+            p = jnp.where(hit, logit, 0.0)
+            sum_e = sum_e + jnp.sum(e.reshape(TILE // 8, 8, 4 * CAP), axis=0)
+            sum_p = sum_p + jnp.sum(p.reshape(TILE // 8, 8, 4 * CAP), axis=0)
+        acc_e[k] = sum_e
+        acc_p[k] = sum_p
 
     def steps(ks, js):
         for j in js:
             lax.fori_loop(ks[0], ks[1], lambda k, carry: (step(k, j), carry)[1], 0)
 
+    def settle(ref, sem):
+        pltpu.make_async_copy(ref, ref, sem).wait()
+
     def arrived(k):
-        for a in range(4):
-            if 4 * k + a != SELF:
-                rows[4 * k + a].wait_recv()
+        settle(rcv.at[pl.ds(4 * k, 4 if k < 7 else 3)], row_rs.at[k])
 
     def z_arrived(d):
-        for q in range(4):
-            z_copies[d, q].wait_recv()
+        settle(kern.at[d], z_rs.at[d - 1])
 
     losses = {}
 
@@ -264,20 +274,17 @@
                 ret[o] = jnp.broadcast_to(loss[:, (a // 2) * LANES : (a // 2 + 1) * LANES], (8, LANES))
             else:
                 losses[o] = pltpu.make_async_remote_copy(
-                    src_ref=lsnd.at[o // 2], dst_ref=ret.at[o], send_sem=loss_ss.at[o],
-                    recv_sem=loss_rs.at[o], device_id=row_source(o), device_id_type=MESH,
+                    src_ref=lsnd.at[o // 2], dst_ref=ret.at[o], send_sem=loss_ss,
+                    recv_sem=loss_rs, device_id=row_source(o), device_id_type=MESH,
                 )
                 losses[o].start()
 
-    for k in range(4):
+    for k in range(6):
         arrived(k)
         steps((k, k + 1), (0,))
     z_arrived(1)
     z_arrived(3)
-    steps((0, 4), (1, 3))
-    for k in range(4, 6):
-        arrived(k)
-        steps((k, k + 1), (0, 1, 3))
+    steps((0, 6), (1, 3))
     z_arrived(2)
     steps((0, 6), (2,))
     for k in range(6):
@@ -287,31 +294,33 @@
         steps((k, k + 1), (0, 1, 3, 2))
         finish(k)
 
+    settle(snd.at[pl.ds(0, SLOTS - 1)], row_ss)
+    settle(kern.at[pl.ds(1, 3)], z_ss)
     at = (order & 1) * CAP + rank
+    settle(ret.at[pl.ds(0, SLOTS - 1)], loss_rs)
     loss_out = jnp.zeros((8, LANES), jnp.float32)
     for o in range(SLOTS):
-        if o != SELF:
-            losses[o].wait_recv()
         mine = jnp.take_along_axis(ret[o], at, axis=1)
         loss_out = jnp.where(order == o, mine, loss_out)
     out_ref[...] = loss_out
-
-    for copy in [*rows.values(), *z_copies.values(), *losses.values()]:
-        copy.wait_send()
+    settle(ret.at[pl.ds(0, SLOTS - 1)], loss_ss)
 
 
 def body(features, tenant, label, tenant_slot, sample, centres):
     vmem = pl.BlockSpec(memory_space=pltpu.VMEM)
-    smem = pl.BlockSpec(memory_space=pltpu.SMEM)
-    hbm = pl.BlockSpec(memory_space=pl.ANY)
+    hbm = pl.BlockSpec(memory_space=pltpu.HBM)
     bf16, f32 = jnp.bfloat16, jnp.float32
     dma = pltpu.SemaphoreType.DMA
     out = pl.pallas_call(
         kernel,
         out_shape=jax.ShapeDtypeStruct((8, LANES), f32),
-        in_specs=[smem, smem, vmem, vmem, hbm, hbm],
+        in_specs=[hbm] * 6,
         out_specs=vmem,
         scratch_shapes=[
+            pltpu.SMEM((SLOTS,), jnp.int32),
+            pltpu.SMEM((4,), jnp.int32),
+            pltpu.VMEM((8, LANES), jnp.int32),
+            pltpu.VMEM((8, LANES), jnp.int32),
             *[pltpu.VMEM((8, TILE, WIDTH), bf16) for _ in range(4)],
             pltpu.VMEM((ROWS, WIDTH), bf16),
             pltpu.VMEM((SLOTS, BLOCK, LANES), bf16),
@@ -322,11 +331,10 @@
             pltpu.VMEM((8, 8, 4 * CAP), f32),
             pltpu.VMEM((16, 8, LANES), f32),
             pltpu.VMEM((SLOTS, 8, LANES), f32),
-            dma((5,)), dma((SLOTS,)), dma((SLOTS,)), dma((3,)), dma((3,)),
-            dma((3, 4)), dma((3, 4)), dma((SLOTS,)), dma((SLOTS,)),
+            dma((9,)), dma, dma((8,)), dma((3,)), dma((3,)), dma, dma((3,)), dma, dma,
         ],
         compiler_params=pltpu.CompilerParams(
-            collective_id=0, has_side_effects=True, vmem_limit_bytes=48 << 20
+            collective_id=0, has_side_effects=True, vmem_limit_bytes=60 << 20
         ),
     )(
         tenant_slot, sample.reshape(4), tenant.reshape(8, LANES), label.reshape(8, LANES),

time: 66.8 us -> 52.5 us (0.79)
  Pallas kernels: 59.8 us -> 51.1 us
  local copies, waits for them, and re-layouts: 6.69 us -> 1.28 us
    pallas_call x1, Pallas kernels: 59.8 us -> 51.1 us  [body(): pl.pallas_call(kernel, out_shape=jax.ShapeDtypeStruct((8, LANES), f32), i...]
    unnamed x13 -> x1, local copies, waits for them, and re-layouts: 6.69 us -> 1.28 us
where the time goes in v2:
time: 52.5 us; the launch traced here: 52.4 us
  Pallas kernels  51.1 us (97%)
  local copies, waits for them, and re-layouts  1.28 us (2%)
    pallas_call x1, Pallas kernels, body(): pl.pallas_call(kernel, out_shape=jax.ShapeDtypeStruct((8, LANES), f32), i...  51.1 us
    unnamed x1, local copies, waits for them, and re-layouts  1.28 us

profile of v2, /device:TPU:1, one launch (start us, length us, event | category | flops | bytes accessed | tf_op | source)
XLA Modules:
  0.0 52.4 jit_solution(13800810618243845657)
XLA Ops:
  0.0 51.1 %shard_map.64 = f32[8,128]{1,0:T(8,128)} custom-call(s32[32]{0:T(128)} %slot_hbm.1, s32[4]{0:T(128)} %bitcast.9, s32[8,128]{1,0:T(8,128)} %bitcast.7, s32[8,128]{1,0:T(8,128)} %bitcast.8, bf16[1024,512]{1,0:T(8,128)(2,1)} %feat_hbm.1, bf16[4,8,128,512]{3,2,1,0:T(8,128)(2,1)} %bitcast.5), custom_call_target="tpu_custom_call" | custom-call | tf_op jit(solution)/shard_map/pallas_call | solution.py:314
  51.1 1.3 %copy.8 = f32[1024]{0:T(1024)} copy(f32[1024]{0:T(1024)} %bitcast.6) | data formatting | bytes 8192

commit v3 on v2

--- a/solution.py
+++ b/solution.py
@@ -13,8 +13,7 @@
 CAP = 64
 SLOTS = 32
 LANES = 128
-CODE = 4 * CAP
-BLOCK = CODE + 16
+BLOCK = 4 * CAP
 logit_scale = 32.0
 margin = 0.35
 epsilon = 1e-06
@@ -31,6 +30,7 @@
 )
 SELF_CHIP = CHIPS.index((0, 0))
 SELF = 2 * SELF_CHIP
+WINDOW = 4
 
 
 def normalized(values, scale):
@@ -41,8 +41,8 @@
 
 def kernel(
     slot_hbm, sample_hbm, tenant_hbm, label_hbm, feat_hbm, cent_hbm, out_ref,
-    slot_ref, sample_ref, tenant_ref, label_ref, cent0, cent1, cent2, cent3, unit, snd, rcv, tiles, kern, acc_e, acc_p, lsnd, ret,
-    in_sem, row_ss, row_rs, quad_ss, quad_rs, z_ss, z_rs, loss_ss, loss_rs,
+    slot_ref, sample_ref, tenant_ref, label_ref, cent0, cent1, cent2, cent3, unit, snd, rcv, tiles, kern, acc_e, acc_p, lsnd, ret, lab_snd, lab_rcv,
+    ready, in_sem, row_ss, row_rs, lab_ss, lab_rs, quad_ss, quad_rs, z_ss, z_rs, loss_ss, loss_rs,
 ):
     group, blk = lax.axis_index("group"), lax.axis_index("blk")
     y, xh = lax.div(group, 2), lax.rem(group, 2)
@@ -67,30 +67,74 @@
         return device(x, y, lax.rem(z + d, 4), c)
 
     cents = (cent0, cent1, cent2, cent3)
-    loads = []
+    owners = [lax.rem(xl + q // 2, 2) * 2 + lax.rem(c + q % 2, 2) for q in range(4)]
+    sample_load = pltpu.make_async_copy(sample_hbm, sample_ref, in_sem.at[5])
+    loads = [
+        pltpu.make_async_copy(cent_hbm.at[owners[q]], cents[q], in_sem.at[q]) for q in range(4)
+    ]
     small = [
-        pltpu.make_async_copy(sample_hbm, sample_ref, in_sem.at[5]),
         pltpu.make_async_copy(slot_hbm, slot_ref, in_sem.at[6]),
         pltpu.make_async_copy(tenant_hbm, tenant_ref, in_sem.at[7]),
         pltpu.make_async_copy(label_hbm, label_ref, in_sem.at[8]),
     ]
+    feat_load = pltpu.make_async_copy(feat_hbm, unit, in_sem.at[4])
+    sample_load.start()
+    loads[2].start()
+    loads[3].start()
+
+    barrier = pltpu.get_barrier_semaphore()
+    along_x = [(dx, dc) for dx in range(4) for dc in range(2) if dx or dc]
+    for dx, dc in along_x:
+        peer = device(lax.rem(x + dx, 4), y, z, lax.rem(c + dc, 2))
+        pl.semaphore_signal(barrier, inc=1, device_id=peer, device_id_type=MESH)
+    y_peers = [device(x, lax.rem(y + d, 4), z, c) for d in (1, 2, 3)]
+    for peer in y_peers + [z_peer(d) for d in (1, 2, 3)]:
+        pl.semaphore_signal(barrier, inc=1, device_id=peer, device_id_type=MESH)
+    for load in [*small, feat_load, loads[0], loads[1]]:
+        load.start()
+
+    quad = {}
+    z_copies = {}
+
+    def along_z(q):
+        for d in (1, 3, 2):
+            z_copies[d, q] = pltpu.make_async_remote_copy(
+                src_ref=kern.at[0, q], dst_ref=kern.at[d, q], send_sem=z_ss,
+                recv_sem=z_rs.at[d - 1, q // 2], device_id=z_peer(d), device_id_type=MESH,
+            )
+            z_copies[d, q].start()
+
+    def own_tile(q):
+        loads[q].wait()
+        block = normalized(cents[q][sample_ref[owners[q]]], logit_scale)
+        if q == 0:
+            kern[0, 0] = block
+        else:
+            tiles[q - 1] = block
+
+    def send_tile(q):
+        if q == 0:
+            along_z(0)
+            return
+        quad[q] = pltpu.make_async_remote_copy(
+            src_ref=tiles.at[q - 1], dst_ref=kern.at[0, q], send_sem=quad_ss.at[q - 1],
+            recv_sem=quad_rs.at[q - 1], device_id=quad_peer(q), device_id_type=MESH,
+        )
+        quad[q].start()
+
+    sample_load.wait()
+    own_tile(2)
+    own_tile(3)
+    pl.semaphore_wait(barrier, len(along_x) + 6)
+    for peer in y_peers:
+        pl.semaphore_signal(ready, inc=1, device_id=peer, device_id_type=MESH)
+    send_tile(2)
+    send_tile(3)
+    for q in (0, 1):
+        own_tile(q)
+        send_tile(q)
+
     for load in small:
-        load.start()
-    for q in range(4):
-        t = lax.rem(xl + q // 2, 2) * 2 + lax.rem(c + q % 2, 2)
-        loads.append(pltpu.make_async_copy(cent_hbm.at[t], cents[q], in_sem.at[q]))
-        loads[q].start()
-    feat_load = pltpu.make_async_copy(feat_hbm, unit, in_sem.at[4])
-    feat_load.start()
-
-    barrier = pltpu.get_barrier_semaphore()
-    others = [o for o in range(SLOTS) if o != SELF]
-    for o in others:
-        pl.semaphore_signal(barrier, inc=1, device_id=row_peer(o), device_id_type=MESH)
-    for d in (1, 2, 3):
-        pl.semaphore_signal(barrier, inc=1, device_id=z_peer(d), device_id_type=MESH)
-
-    for load in small[1:]:
         load.wait()
     tenant = tenant_ref[...]
     slot = jnp.zeros_like(tenant)
@@ -136,42 +180,25 @@
     unit[...] = normalized(unit[...], 1.0)
 
 
-    quad = {}
-    z_copies = {}
-
-    def along_z(q):
-        for d in (1, 3, 2):
-            z_copies[d, q] = pltpu.make_async_remote_copy(
-                src_ref=kern.at[0, q], dst_ref=kern.at[d, q], send_sem=z_ss,
-                recv_sem=z_rs.at[d - 1], device_id=z_peer(d), device_id_type=MESH,
-            )
-            z_copies[d, q].start()
-
-    def own_tiles():
-        small[0].wait()
-        for q in (2, 3, 0, 1):
-            t = lax.rem(xl + q // 2, 2) * 2 + lax.rem(c + q % 2, 2)
-            loads[q].wait()
-            block = normalized(cents[q][sample_ref[t]], logit_scale)
-            if q == 0:
-                kern[0, 0] = block
-                along_z(0)
-                continue
-            tiles[q - 1] = block
-            quad[q] = pltpu.make_async_remote_copy(
-                src_ref=tiles.at[q - 1], dst_ref=kern.at[0, q], send_sem=quad_ss.at[q - 1],
-                recv_sem=quad_rs.at[q - 1], device_id=quad_peer(q), device_id_type=MESH,
-            )
-            quad[q].start()
-
-    rows = {}
+    def send_rows(k):
+        for a in (0, 2, 1, 3):
+            o = 4 * k + a
+            if o != SELF:
+                pltpu.make_async_remote_copy(
+                    src_ref=snd.at[o], dst_ref=rcv.at[o], send_sem=row_ss,
+                    recv_sem=row_rs.at[k], device_id=row_peer(o), device_id_type=MESH,
+                ).start()
+
     iota_slot = lax.broadcasted_iota(jnp.int32, (4 * CAP, 1), 0)
     for k in range(8):
         placing = (position_row == iota_slot + k * 4 * CAP).astype(jnp.float32).astype(jnp.bfloat16)
         placed = jnp.dot(placing, unit[...], preferred_element_type=jnp.float32).astype(jnp.bfloat16)
         coded = lax.dot_general(
             codes, placing, (((1,), (1,)), ((), ())), preferred_element_type=jnp.float32
-        ).astype(jnp.bfloat16)
+        )
+        classes = coded[0:1, :] * float(TILE) + coded[1:2, :]
+        for h in range(2):
+            lab_snd[2 * k + h] = classes[:, h * LANES : (h + 1) * LANES]
         for a in range(4):
             o = 4 * k + a
             to = rcv if o == SELF else snd
@@ -179,19 +206,19 @@
                 to[o, f * CAP : (f + 1) * CAP, :] = placed[
                     a * CAP : (a + 1) * CAP, f * LANES : (f + 1) * LANES
                 ]
-            to[o, CODE:BLOCK, :] = coded[:, (a // 2) * LANES : (a // 2 + 1) * LANES]
         if k == 0:
-            pl.semaphore_wait(barrier, len(others) + 3)
-        for a in (0, 2, 1, 3):
+            pl.semaphore_wait(ready, 3)
+        if k < WINDOW:
+            send_rows(k)
+        for a in range(4):
             o = 4 * k + a
-            if o != SELF:
-                rows[o] = pltpu.make_async_remote_copy(
-                    src_ref=snd.at[o], dst_ref=rcv.at[o], send_sem=row_ss,
-                    recv_sem=row_rs.at[k], device_id=row_peer(o), device_id_type=MESH,
-                )
-                rows[o].start()
-        if k == 0:
-            own_tiles()
+            if o == SELF:
+                lab_rcv[o] = classes[:, (a // 2) * LANES : (a // 2 + 1) * LANES]
+            else:
+                pltpu.make_async_remote_copy(
+                    src_ref=lab_snd.at[o // 2], dst_ref=lab_rcv.at[o], send_sem=lab_ss,
+                    recv_sem=lab_rs.at[k], device_id=row_peer(o), device_id_type=MESH,
+                ).start()
         if k == 1:
             quad[1].wait()
             along_z(1)
@@ -210,10 +237,8 @@
     def targets(k):
         halves = []
         for h in range(2):
-            first = rcv[4 * k + 2 * h, CODE:BLOCK, :].astype(jnp.float32)
-            second = rcv[4 * k + 2 * h + 1, CODE:BLOCK, :].astype(jnp.float32)
-            both = jnp.where(lane < CAP, first, second)
-            halves.append(both[0:1, :] * float(TILE) + both[1:2, :])
+            first, second = lab_rcv[4 * k + 2 * h], lab_rcv[4 * k + 2 * h + 1]
+            halves.append(jnp.where(lane < CAP, first, second))
         return jnp.concatenate(halves, axis=1)
 
     def group_rows(k):
@@ -227,17 +252,18 @@
             axis=0,
         )
 
-    def step(k, j):
+    def step(k, j, halves):
         target = targets(k)
         block = group_rows(k)
 
-        logits = lax.dot_general(
-            kern[j].reshape(4 * TILE, WIDTH), block, (((1,), (1,)), ((), ())),
-            preferred_element_type=jnp.float32,
-        )
         sum_e, sum_p = acc_e[k], acc_p[k]
-        for q in range(4):
-            logit = logits[q * TILE : (q + 1) * TILE]
+        for q in [2 * h + a for h in halves for a in range(2)]:
+            if q % 2 == 0:
+                logits = lax.dot_general(
+                    kern[j, q : q + 2].reshape(2 * TILE, WIDTH), block,
+                    (((1,), (1,)), ((), ())), preferred_element_type=jnp.float32,
+                )
+            logit = logits[q % 2 * TILE : (q % 2 + 1) * TILE]
             owner = (lax.rem(xl + q // 2, 2) * 4 + lax.rem(z - j + 4, 4)) * 2 + lax.rem(c + q % 2, 2)
             hit = in_tile == target - (owner * TILE).astype(jnp.float32)
             e = jnp.where(hit, 0.0, jnp.exp2(logit * LOG2E))
@@ -247,18 +273,24 @@
         acc_e[k] = sum_e
         acc_p[k] = sum_p
 
-    def steps(ks, js):
-        for j in js:
-            lax.fori_loop(ks[0], ks[1], lambda k, carry: (step(k, j), carry)[1], 0)
+    def steps(ks, js, halves=(0, 1)):
+        def one(k, carry):
+            for j in js:
+                step(k, j, halves)
+            return carry
+
+        lax.fori_loop(ks[0], ks[1], one, 0)
 
     def settle(ref, sem):
         pltpu.make_async_copy(ref, ref, sem).wait()
 
     def arrived(k):
-        settle(rcv.at[pl.ds(4 * k, 4 if k < 7 else 3)], row_rs.at[k])
-
-    def z_arrived(d):
-        settle(kern.at[d], z_rs.at[d - 1])
+        n = 4 if k < 7 else 3
+        settle(lab_rcv.at[pl.ds(4 * k, n)], lab_rs.at[k])
+        settle(rcv.at[pl.ds(4 * k, n)], row_rs.at[k])
+
+    def z_arrived(d, h):
+        settle(kern.at[d, pl.ds(2 * h, 2)], z_rs.at[d - 1, h])
 
     losses = {}
 
@@ -267,11 +299,11 @@
         total = jnp.sum(acc_e[k], axis=0, keepdims=True) + jnp.exp(positive)
         loss = jnp.log(total) - positive
         for h in range(2):
-            lsnd[2 * k + h] = jnp.broadcast_to(loss[:, h * LANES : (h + 1) * LANES], (8, LANES))
+            lsnd[2 * k + h] = loss[:, h * LANES : (h + 1) * LANES]
         for a in range(4):
             o = 4 * k + a
             if o == SELF:
-                ret[o] = jnp.broadcast_to(loss[:, (a // 2) * LANES : (a // 2 + 1) * LANES], (8, LANES))
+                ret[o] = loss[:, (a // 2) * LANES : (a // 2 + 1) * LANES]
             else:
                 losses[o] = pltpu.make_async_remote_copy(
                     src_ref=lsnd.at[o // 2], dst_ref=ret.at[o], send_sem=loss_ss,
@@ -279,28 +311,35 @@
                 )
                 losses[o].start()
 
-    for k in range(6):
+    def next_rows(k):
         arrived(k)
+        if k + WINDOW < 8:
+            send_rows(k + WINDOW)
+
+    for k in range(4):
+        next_rows(k)
         steps((k, k + 1), (0,))
-    z_arrived(1)
-    z_arrived(3)
-    steps((0, 6), (1, 3))
-    z_arrived(2)
-    steps((0, 6), (2,))
-    for k in range(6):
+    for d in (1, 3, 2):
+        z_arrived(d, 0)
+    steps((0, 4), (1, 3, 2), (0,))
+    for d in (1, 3, 2):
+        z_arrived(d, 1)
+    steps((0, 4), (1, 3, 2), (1,))
+    for k in range(4):
         finish(k)
-    for k in range(6, 8):
-        arrived(k)
+    for k in range(4, 8):
+        next_rows(k)
         steps((k, k + 1), (0, 1, 3, 2))
         finish(k)
 
     settle(snd.at[pl.ds(0, SLOTS - 1)], row_ss)
+    settle(lab_rcv.at[pl.ds(0, SLOTS - 1)], lab_ss)
     settle(kern.at[pl.ds(1, 3)], z_ss)
     at = (order & 1) * CAP + rank
     settle(ret.at[pl.ds(0, SLOTS - 1)], loss_rs)
     loss_out = jnp.zeros((8, LANES), jnp.float32)
     for o in range(SLOTS):
-        mine = jnp.take_along_axis(ret[o], at, axis=1)
+        mine = jnp.take_along_axis(jnp.broadcast_to(ret[o], (8, LANES)), at, axis=1)
         loss_out = jnp.where(order == o, mine, loss_out)
     out_ref[...] = loss_out
     settle(ret.at[pl.ds(0, SLOTS - 1)], loss_ss)
@@ -329,9 +368,12 @@
             pltpu.VMEM((4, 4, TILE, WIDTH), bf16),
             pltpu.VMEM((8, 8, 4 * CAP), f32),
             pltpu.VMEM((8, 8, 4 * CAP), f32),
-            pltpu.VMEM((16, 8, LANES), f32),
-            pltpu.VMEM((SLOTS, 8, LANES), f32),
-            dma((9,)), dma, dma((8,)), dma((3,)), dma((3,)), dma, dma((3,)), dma, dma,
+            pltpu.VMEM((16, 1, LANES), f32),
+            pltpu.VMEM((SLOTS, 1, LANES), f32),
+            pltpu.VMEM((16, 1, LANES), f32),
+            pltpu.VMEM((SLOTS, 1, LANES), f32),
+            pltpu.SemaphoreType.REGULAR,
+            dma((9,)), dma, dma((8,)), dma, dma((8,)), dma((3,)), dma((3,)), dma, dma((3, 2)), dma, dma,
         ],
         compiler_params=pltpu.CompilerParams(
             collective_id=0, has_side_effects=True, vmem_limit_bytes=60 << 20

time: 52.5 us -> 45.2 us (0.86)
  Pallas kernels: 51.1 us -> 43.8 us
    pallas_call x1, Pallas kernels: 51.1 us -> 43.8 us  [body(): pl.pallas_call(kernel, out_shape=jax.ShapeDtypeStruct((8, LANES), f32), i...]
where the time goes in v3:
time: 45.2 us; the launch traced here: 45.1 us
  Pallas kernels  43.8 us (97%)
  local copies, waits for them, and re-layouts  1.28 us (3%)
    pallas_call x1, Pallas kernels, body(): pl.pallas_call(kernel, out_shape=jax.ShapeDtypeStruct((8, LANES), f32), i...  43.8 us
    unnamed x1, local copies, waits for them, and re-layouts  1.28 us

profile of v3, /device:TPU:1, one launch (start us, length us, event | category | flops | bytes accessed | tf_op | source)
XLA Modules:
  0.0 45.1 jit_solution(2939079700620383552)
XLA Ops:
  0.0 43.8 %shard_map.64 = f32[8,128]{1,0:T(8,128)} custom-call(s32[32]{0:T(128)} %slot_hbm.1, s32[4]{0:T(128)} %bitcast.9, s32[8,128]{1,0:T(8,128)} %bitcast.7, s32[8,128]{1,0:T(8,128)} %bitcast.8, bf16[1024,512]{1,0:T(8,128)(2,1)} %feat_hbm.1, bf16[4,8,128,512]{3,2,1,0:T(8,128)(2,1)} %bitcast.5), custom_call_target="tpu_custom_call" | custom-call | tf_op jit(solution)/shard_map/pallas_call | solution.py:353
  43.8 1.3 %copy.8 = f32[1024]{0:T(1024)} copy(f32[1024]{0:T(1024)} %bitcast.6) | data formatting | bytes 8192

commit v4 on v3

--- a/solution.py
+++ b/solution.py
@@ -123,17 +123,8 @@
         quad[q].start()
 
     sample_load.wait()
-    own_tile(2)
-    own_tile(3)
-    pl.semaphore_wait(barrier, len(along_x) + 6)
-    for peer in y_peers:
-        pl.semaphore_signal(ready, inc=1, device_id=peer, device_id_type=MESH)
-    send_tile(2)
-    send_tile(3)
-    for q in (0, 1):
+    for q in (2, 3, 0, 1):
         own_tile(q)
-        send_tile(q)
-
     for load in small:
         load.wait()
     tenant = tenant_ref[...]
@@ -180,6 +171,14 @@
     unit[...] = normalized(unit[...], 1.0)
 
 
+    pl.semaphore_wait(barrier, len(along_x) + 6)
+    for peer in y_peers:
+        pl.semaphore_signal(ready, inc=1, device_id=peer, device_id_type=MESH)
+    send_tile(2)
+    send_tile(3)
+    for q in (0, 1):
+        send_tile(q)
+
     def send_rows(k):
         for a in (0, 2, 1, 3):
             o = 4 * k + a
@@ -208,8 +207,6 @@
                 ]
         if k == 0:
             pl.semaphore_wait(ready, 3)
-        if k < WINDOW:
-            send_rows(k)
         for a in range(4):
             o = 4 * k + a
             if o == SELF:
@@ -219,6 +216,8 @@
                     src_ref=lab_snd.at[o // 2], dst_ref=lab_rcv.at[o], send_sem=lab_ss,
                     recv_sem=lab_rs.at[k], device_id=row_peer(o), device_id_type=MESH,
                 ).start()
+        if k < WINDOW:
+            send_rows(k)
         if k == 1:
             quad[1].wait()
             along_z(1)
@@ -307,7 +306,7 @@
             else:
                 losses[o] = pltpu.make_async_remote_copy(
                     src_ref=lsnd.at[o // 2], dst_ref=ret.at[o], send_sem=loss_ss,
-                    recv_sem=loss_rs, device_id=row_source(o), device_id_type=MESH,
+                    recv_sem=loss_rs.at[k], device_id=row_source(o), device_id_type=MESH,
                 )
                 losses[o].start()
 
@@ -336,9 +335,10 @@
     settle(lab_rcv.at[pl.ds(0, SLOTS - 1)], lab_ss)
     settle(kern.at[pl.ds(1, 3)], z_ss)
     at = (order & 1) * CAP + rank
-    settle(ret.at[pl.ds(0, SLOTS - 1)], loss_rs)
     loss_out = jnp.zeros((8, LANES), jnp.float32)
     for o in range(SLOTS):
+        if o % 4 == 0:
+            settle(ret.at[pl.ds(o, 4 if o < 28 else 3)], loss_rs.at[o // 4])
         mine = jnp.take_along_axis(jnp.broadcast_to(ret[o], (8, LANES)), at, axis=1)
         loss_out = jnp.where(order == o, mine, loss_out)
     out_ref[...] = loss_out
@@ -373,7 +373,7 @@
             pltpu.VMEM((16, 1, LANES), f32),
             pltpu.VMEM((SLOTS, 1, LANES), f32),
             pltpu.SemaphoreType.REGULAR,
-            dma((9,)), dma, dma((8,)), dma, dma((8,)), dma((3,)), dma((3,)), dma, dma((3, 2)), dma, dma,
+            dma((9,)), dma, dma((8,)), dma, dma((8,)), dma((3,)), dma((3,)), dma, dma((3, 2)), dma, dma((8,)),
         ],
         compiler_params=pltpu.CompilerParams(
             collective_id=0, has_side_effects=True, vmem_limit_bytes=60 << 20

time: 45.2 us -> 44.5 us (0.985)
  Pallas kernels: 43.8 us -> 43.1 us
    pallas_call x1, Pallas kernels: 43.8 us -> 43.1 us  [body(): pl.pallas_call(kernel, out_shape=jax.ShapeDtypeStruct((8, LANES), f32), i...]
where the time goes in v4:
time: 44.5 us; the launch traced here: 44.4 us
  Pallas kernels  43.1 us (97%)
  local copies, waits for them, and re-layouts  1.28 us (3%)
    pallas_call x1, Pallas kernels, body(): pl.pallas_call(kernel, out_shape=jax.ShapeDtypeStruct((8, LANES), f32), i...  43.1 us
    unnamed x1, local copies, waits for them, and re-layouts  1.28 us

profile of v4, /device:TPU:1, one launch (start us, length us, event | category | flops | bytes accessed | tf_op | source)
XLA Modules:
  0.0 44.4 jit_solution(8431901004354181712)
XLA Ops:
  0.0 43.1 %shard_map.64 = f32[8,128]{1,0:T(8,128)} custom-call(s32[32]{0:T(128)} %slot_hbm.1, s32[4]{0:T(128)} %bitcast.9, s32[8,128]{1,0:T(8,128)} %bitcast.7, s32[8,128]{1,0:T(8,128)} %bitcast.8, bf16[1024,512]{1,0:T(8,128)(2,1)} %feat_hbm.1, bf16[4,8,128,512]{3,2,1,0:T(8,128)(2,1)} %bitcast.5), custom_call_target="tpu_custom_call" | custom-call | tf_op jit(solution)/shard_map/pallas_call | solution.py:353
  43.1 1.3 %copy.8 = f32[1024]{0:T(1024)} copy(f32[1024]{0:T(1024)} %bitcast.6) | data formatting | bytes 8192

commit v5 on v4

--- a/solution.py
+++ b/solution.py
@@ -24,10 +24,7 @@
     return min(d, 4 - d)
 
 
-CHIPS = sorted(
-    [(dx, dy) for dx in range(4) for dy in range(4)],
-    key=lambda d: (-hops(d[0]) - hops(d[1]), (d[0] + d[1]) % 4),
-)
+CHIPS = [(2, 2), (1, 2), (2, 1), (1, 1), (1, 3), (2, 3), (3, 2), (3, 3), (3, 1), (2, 0), (0, 2), (1, 0), (0, 1), (3, 0), (0, 3), (0, 0)]
 SELF_CHIP = CHIPS.index((0, 0))
 SELF = 2 * SELF_CHIP
 WINDOW = 4
@@ -54,11 +51,12 @@
 
     def row_peer(o):
         dx, dy = CHIPS[o // 2]
-        return device(lax.rem(x + dx, 4), lax.rem(y + dy, 4), z, lax.rem(c + o % 2, 2))
+        return device(lax.rem(x + dx + 2 * c * (4 - dx), 4), lax.rem(y + dy + 2 * c * (4 - dy), 4), z, lax.rem(c + o % 2, 2))
 
     def row_source(o):
         dx, dy = CHIPS[o // 2]
-        return device(lax.rem(x + 4 - dx, 4), lax.rem(y + 4 - dy, 4), z, lax.rem(c + o % 2, 2))
+        sc = lax.rem(c + o % 2, 2)
+        return device(lax.rem(x + 4 - dx + 2 * sc * dx, 4), lax.rem(y + 4 - dy + 2 * sc * dy, 4), z, sc)
 
     def quad_peer(q):
         return device(xh * 2 + lax.rem(xl + q // 2, 2), y, z, lax.rem(c + q % 2, 2))
@@ -133,7 +131,8 @@
         slot = jnp.where(tenant == n, slot_ref[n], slot)
     y_to, xh_to = lax.shift_right_logical(slot, 3), lax.shift_right_logical(slot, 2) & 1
     x_to, c_to = xh_to * 2 + (lax.shift_right_logical(slot, 1) & 1), slot & 1
-    dx, dy, dc = (x_to - x + 4) & 3, (y_to - y + 4) & 3, (c_to + c) & 1
+    turn = 1 - 2 * c
+    dx, dy, dc = (turn * (x_to - x) + 4) & 3, (turn * (y_to - y) + 4) & 3, (c_to + c) & 1
     chip = jnp.zeros_like(slot)
     for n, (a, b) in enumerate(CHIPS):
         chip = jnp.where((dx == a) & (dy == b), n, chip)

time: 44.5 us -> 46.9 us (1.054)
  Pallas kernels: 43.1 us -> 45.5 us
    pallas_call x1, Pallas kernels: 43.1 us -> 45.5 us  [body(): pl.pallas_call(kernel, out_shape=jax.ShapeDtypeStruct((8, LANES), f32), i...]
where the time goes in v5:
time: 46.9 us; the launch traced here: 46.8 us
  Pallas kernels  45.5 us (97%)
  local copies, waits for them, and re-layouts  1.28 us (3%)
    pallas_call x1, Pallas kernels, body(): pl.pallas_call(kernel, out_shape=jax.ShapeDtypeStruct((8, LANES), f32), i...  45.5 us
    unnamed x1, local copies, waits for them, and re-layouts  1.28 us

profile of v5, /device:TPU:1, one launch (start us, length us, event | category | flops | bytes accessed | tf_op | source)
XLA Modules:
  0.0 46.8 jit_solution(12843663231609954084)
XLA Ops:
  0.0 45.5 %shard_map.64 = f32[8,128]{1,0:T(8,128)} custom-call(s32[32]{0:T(128)} %slot_hbm.1, s32[4]{0:T(128)} %bitcast.9, s32[8,128]{1,0:T(8,128)} %bitcast.7, s32[8,128]{1,0:T(8,128)} %bitcast.8, bf16[1024,512]{1,0:T(8,128)(2,1)} %feat_hbm.1, bf16[4,8,128,512]{3,2,1,0:T(8,128)(2,1)} %bitcast.5), custom_call_target="tpu_custom_call" | custom-call | tf_op jit(solution)/shard_map/pallas_call | solution.py:352
  45.5 1.3 %copy.8 = f32[1024]{0:T(1024)} copy(f32[1024]{0:T(1024)} %bitcast.6) | data formatting | bytes 8192
